TPU v7x, 256 devices: a whole 4x4x8 slice. The times are simulated.
256 devices in a mesh: gx: 16 (over x, y_lo, core), gy: 16 (over y_hi, z).
Axes of the slice: x: 4, y: 4 (y_hi: 2, y_lo: 2; y = y_hi * 2 + y_lo), z: 8, core: 2. Of those that a mesh axis runs over, the one named last changes fastest.
Arguments:
- tokens: bfloat16 [512, 8192], P('gy', 'gx'), may hold values from -6 to 6
- gate_first: bfloat16 [8192, 28672], P('gx', 'gy'), may hold values from -0.0625 to 0.0625
- up_first: bfloat16 [8192, 28672], P('gx', 'gy'), may hold values from -0.0625 to 0.0625
- down_first: bfloat16 [28672, 8192], P('gy', 'gx'), may hold values from -0.0625 to 0.0625
- gate_second: bfloat16 [8192, 28672], P('gx', 'gy'), may hold values from -0.0625 to 0.0625
- up_second: bfloat16 [8192, 28672], P('gx', 'gy'), may hold values from -0.0625 to 0.0625
- down_second: bfloat16 [28672, 8192], P('gy', 'gx'), may hold values from -0.0625 to 0.0625
Outputs:
- second_out: float32 [512, 8192], P('gy', 'gx')
All inputs are finite; a program needn't handle non-finite values.
Results may differ from a plain program's by a relative error of at most 0.0085.
Values may be sent and summed in bfloat16 or wider, within the bound.
A program may use at most 64 MiB of HBM per device.

v0:
```python
import jax
import jax.numpy as jnp
from jax import lax
from jax.sharding import PartitionSpec as P


def hidden_units(gathered, gate_weight, up_weight):
    width = gate_weight.shape[1]
    gate_part = jnp.dot(gathered, gate_weight, preferred_element_type=jnp.float32)
    up_part = jnp.dot(gathered, up_weight, preferred_element_type=jnp.float32)
    summed = lax.psum_scatter(
        jnp.concatenate([gate_part, up_part], axis=1), "gx", scatter_dimension=0, tiled=True
    )
    gate_sum = summed[:, :width]
    up_sum = summed[:, width:]
    return (jax.nn.silu(gate_sum) * up_sum).astype(jnp.bfloat16)


def down_partial(hidden, down_weight):
    return jnp.dot(
        lax.all_gather(hidden, "gx", axis=0, tiled=True),
        down_weight,
        preferred_element_type=jnp.float32,
    )


def shards(tokens, gate_first, up_first, down_first, gate_second, up_second, down_second):
    gathered = lax.all_gather(tokens, "gy", axis=0, tiled=True)
    hidden = hidden_units(gathered, gate_first, up_first)
    partial_value = down_partial(hidden, down_first)
    own_rows = lax.psum_scatter(partial_value, "gy", scatter_dimension=0, tiled=True).astype(
        jnp.bfloat16
    )
    gathered = lax.all_gather(own_rows, "gy", axis=0, tiled=True)
    hidden = hidden_units(gathered, gate_second, up_second)
    partial_value = down_partial(hidden, down_second)
    return lax.psum_scatter(partial_value, "gy", scatter_dimension=0, tiled=True)


def solution(mesh):
    in_specs = (
        P("gy", "gx"),
        P("gx", "gy"),
        P("gx", "gy"),
        P("gy", "gx"),
        P("gx", "gy"),
        P("gx", "gy"),
        P("gy", "gx"),
    )
    out_specs = P("gy", "gx")
    return jax.shard_map(shards, mesh=mesh, in_specs=in_specs, out_specs=out_specs, check_vma=False)
```

profile of v0, /device:TPU:1, one launch (start us, length us, event | category | flops | bytes accessed | tf_op | source)
XLA Modules:
  0.0 769.4 jit_solution(6632579174537579707)
XLA Ops:
  6.5 0.0 copy-start
  6.5 0.0 reduce-scatter.5.cloned.1.call-start
  6.5 41.0 %all_gather.12 = bf16[512,512]{1,0:T(8,128)(2,1)S(1)} all-gather(bf16[32,512]{1,0:T(8,128)(2,1)} %param.7), channel_id=1, replica_groups=mesh['gx'=16,'gy'=16] {'gy'}, dimensions={0}, use_global_device_ids=true | all-gather | bytes 557056 | tf_op jit(solution)/shard_map/all_gather | solution.py:28
  47.5 0.0 copy-done
  47.5 0.0 copy-start.1
  47.5 1.1 fusion.3
  48.7 0.4 copy-done.1
  49.0 1.1 fusion.2
  50.2 4.0 pad_maximum_fusion
  54.2 0.0 reduce-scatter.5.cloned.1.call-update
  54.2 0.0 all-gather.3.cloned.1.call-start
  54.2 90.0 %reduce-scatter.5.cloned.1.call-done = f32[32,3584]{1,0:T(8,128)} async-done(((f32[512,3584]{1,0:T(8,128)}), f32[32,3584]{1,0:T(8,128)}) %reduce-scatter.5.cloned.1.call-update) | async-done | bytes 458768 | tf_op jit(solution)/shard_map/reduce_scatter | solution.py:11
  144.2 1.8 fusion.1
  146.0 0.0 all-gather.3.cloned.1.call-update
  146.0 0.0 reduce-scatter.7.cloned.1.call-start
  146.0 37.8 %all-gather.3.cloned.1.call-done = bf16[512,1792]{1,0:T(8,128)(2,1)} async-done(((bf16[32,1792]{1,0:T(8,128)(2,1)}), bf16[512,1792]{1,0:T(8,128)(2,1)}) %all-gather.3.cloned.1.call-update) | async-done | bytes 1835024 | tf_op jit(solution)/shard_map/all_gather | solution.py:21
  183.8 4.1 fusion.4
  188.0 0.0 reduce-scatter.7.cloned.1.call-update
  188.0 0.0 reduce-scatter.9.cloned.1.call-start
  188.0 193.6 %reduce-scatter.7.cloned.1.call-done = f32[32,512]{1,0:T(8,128)} async-done(((f32[512,512]{1,0:T(8,128)}), f32[32,512]{1,0:T(8,128)}) %reduce-scatter.7.cloned.1.call-update) | async-done | bytes 65552 | tf_op jit(solution)/shard_map/reduce_scatter | solution.py:31
  381.7 0.8 convert_element_type.10
  382.5 34.4 %all_gather.14 = bf16[512,512]{1,0:T(8,128)(2,1)S(1)} all-gather(bf16[32,512]{1,0:T(8,128)(2,1)S(1)} %convert_element_type.10), channel_id=1, replica_groups=mesh['gx'=16,'gy'=16] {'gy'}, dimensions={0}, use_global_device_ids=true | all-gather | bytes 557056 | tf_op jit(solution)/shard_map/all_gather | solution.py:34
  416.9 0.0 copy-start.2
  416.9 2.7 fusion.6
  419.7 0.0 copy-done.2
  419.7 1.1 fusion.5
  420.8 4.0 pad_maximum_fusion.1
  424.8 0.0 reduce-scatter.9.cloned.1.call-update
  424.8 0.0 all-gather.5.cloned.1.call-start
  424.9 95.6 %reduce-scatter.9.cloned.1.call-done = f32[32,3584]{1,0:T(8,128)} async-done(((f32[512,3584]{1,0:T(8,128)}), f32[32,3584]{1,0:T(8,128)}) %reduce-scatter.9.cloned.1.call-update) | async-done | bytes 458768 | tf_op jit(solution)/shard_map/reduce_scatter | solution.py:11
  520.5 1.8 fusion
  522.2 0.0 all-gather.5.cloned.1.call-update
  522.2 0.0 reduce-scatter.11.cloned.1.call-start
  522.3 38.4 %all-gather.5.cloned.1.call-done = bf16[512,1792]{1,0:T(8,128)(2,1)} async-done(((bf16[32,1792]{1,0:T(8,128)(2,1)}), bf16[512,1792]{1,0:T(8,128)(2,1)}) %all-gather.5.cloned.1.call-update) | async-done | bytes 1835024 | tf_op jit(solution)/shard_map/all_gather | solution.py:21
  560.7 4.1 fusion.7
  564.8 0.0 reduce-scatter.11.cloned.1.call-update
  564.8 197.8 %reduce-scatter.11.cloned.1.call-done = f32[32,512]{1,0:T(8,128)} async-done(((f32[512,512]{1,0:T(8,128)}), f32[32,512]{1,0:T(8,128)}) %reduce-scatter.11.cloned.1.call-update) | async-done | bytes 65552 | tf_op jit(solution)/shard_map/reduce_scatter | solution.py:37
Async XLA Ops:
  6.5 41.0 %copy-start = (bf16[512,1792]{1,0:T(8,128)(2,1)S(1)}, bf16[512,1792]{1,0:T(8,128)(2,1)}, u32[]{:S(2)}) copy-start(bf16[512,1792]{1,0:T(8,128)(2,1)} %param.9) | copy-start | bytes 5505028
  6.5 137.7 %reduce-scatter.5.cloned.1.call-start = ((), (), s32[]{:S(2)}) async-start(), calls=%async_computation.4 | async-start | bytes 7798784 | tf_op jit(solution)/shard_map/reduce_scatter | solution.py:11
  47.5 1.5 copy-start.1
  54.2 129.6 %all-gather.3.cloned.1.call-start = ((), (), s32[]{:S(2)}) async-start(), calls=%async_computation.5 | async-start | bytes 1949696 | tf_op jit(solution)/shard_map/all_gather | solution.py:21
  146.0 235.7 %reduce-scatter.7.cloned.1.call-start = ((), (), s32[]{:S(2)}) async-start(), calls=%async_computation.6 | async-start | bytes 1114112 | tf_op jit(solution)/shard_map/reduce_scatter | solution.py:31
  188.0 332.5 %reduce-scatter.9.cloned.1.call-start = ((), (), s32[]{:S(2)}) async-start(), calls=%async_computation.7 | async-start | bytes 7798784 | tf_op jit(solution)/shard_map/reduce_scatter | solution.py:11
  416.9 2.8 copy-start.2
  424.8 135.8 %all-gather.5.cloned.1.call-start = ((), (), s32[]{:S(2)}) async-start(), calls=%async_computation.8 | async-start | bytes 1949696 | tf_op jit(solution)/shard_map/all_gather | solution.py:21
  522.2 240.4 %reduce-scatter.11.cloned.1.call-start = ((), (), s32[]{:S(2)}) async-start(), calls=%async_computation.9 | async-start | bytes 1114112 | tf_op jit(solution)/shard_map/reduce_scatter | solution.py:37
Sparse Core Ops, SparseCore 0:
  54.3 89.8 reduce-scatter.4
  146.1 37.6 all-gather.2
  188.1 193.4 reduce-scatter.6
  424.9 95.4 reduce-scatter.8
  522.4 38.2 all-gather.4
  564.9 197.6 reduce-scatter.10
where the time goes:
time: 774 us; the launch traced here: 769 us
  waiting for transfers between devices  653 us (84%)
  blocking collectives  75.4 us (10%)
  matrix products  14.4 us (2%)
  between operations  13.5 us (2%)
  other arithmetic  12.4 us (2%)
    reduce_scatter x2, waiting for transfers between devices, shards(): lax.psum_scatter(partial_value, 'gy', scatter_dimension=0, tiled=True)  391 us
    reduce_scatter x2, waiting for transfers between devices, hidden_units(): lax.psum_scatter(jnp.concatenate([gate_part, up_part], axis=1), 'gx', sca...  186 us
    all_gather x2, waiting for transfers between devices, down_partial(): lax.all_gather(hidden, 'gx', axis=0, tiled=True)  76.2 us
    all_gather x1, blocking collectives, shards(): gathered = lax.all_gather(tokens, 'gy', axis=0, tiled=True)  41 us
    all_gather x1, blocking collectives, shards(): gathered = lax.all_gather(own_rows, 'gy', axis=0, tiled=True)  34.4 us
  transfers between devices with their start and end apart: 6, of which 6 were waited for; matrix products, arithmetic and copies ran while one was open for 0% of the time, Pallas kernels for 0%

commit v1 on v0

v1 whole, which is shorter than its diff:
```python
import functools

import jax
import jax.numpy as jnp
from jax import lax
from jax.experimental import pallas as pl
from jax.experimental.pallas import tpu as pltpu
from jax.sharding import PartitionSpec as P

HALVES = 2
ROWS = 16
WIDTH = 512
HIDDEN = 1792
CHUNKS = ((0, 512), (512, 640), (1152, 640))
NC = len(CHUNKS)
OFFSETS = tuple((dx, dy) for dx in range(4) for dy in range(2) if dx + dy > 0)
BF16 = jnp.bfloat16
F32 = jnp.float32


def wait_bytes(ref, sem):
    pltpu.make_async_copy(ref, ref, sem).wait()


def kernel(
    tokens, g0, u0, d0, g1, u1, d1, out,
    wg, wu, wd, tok, part, crecv, rsend, rrecv, hid, acc, zsend, zrecv, ysum, yrecv,
    w_s, c_s, r_s, a_s, f_s, z_s, y_s, t_s, i_s,
):
    gx, gy = lax.axis_index("gx"), lax.axis_index("gy")
    c, chip = lax.rem(gx, 2), gx // 2
    yl, x = lax.rem(chip, 2), chip // 2
    z, yh = lax.rem(gy, 8), gy // 8

    def remote(src, dst, sems, index, device):
        pltpu.make_async_remote_copy(
            src_ref=src, dst_ref=dst, send_sem=sems.at[(0, *index)], recv_sem=sems.at[(1, *index)],
            device_id=device, device_id_type=pl.DeviceIdType.MESH,
        ).start()

    other_core = (chip * 2 + 1 - c, gy)
    other_half = (gx, (1 - yh) * 8 + z)

    def chip_at(dx, dy):
        return lax.rem(x + dx, 4) * 2 + lax.rem(yl + dy, 2)

    def z_at(dz):
        return lax.rem(z + dz, 8)

    for n, (src, dst) in enumerate(
        ((g0, wg.at[0]), (u0, wu.at[0]), (d0, wd.at[0]), (g1, wg.at[1]), (u1, wu.at[1]), (d1, wd.at[1]))
    ):
        pltpu.make_async_copy(src, dst, w_s.at[n]).start()

    def wait_weight(n):
        ref = (wg, wu, wd)[n % 3].at[n // 3]
        wait_bytes(ref, w_s.at[n])

    def first_send(h):
        tok[0, h, yh, z] = tokens[pl.ds(ROWS * h, ROWS), :]
        mine = tok.at[0, h, yh, z]
        remote(mine, mine, i_s, (0, h), other_half)
        for dz in range(1, 8):
            remote(mine, mine, i_s, (1, h), (gx, yh * 8 + z_at(dz)))

    def first_forward(h):
        theirs = tok.at[0, h, 1 - yh, z]
        wait_bytes(theirs, i_s.at[1, 0, h])
        for dz in range(1, 8):
            remote(theirs, theirs, i_s, (2, h), (gx, yh * 8 + z_at(dz)))

    def first_wait(h):
        for n in (1, 2):
            wait_bytes(tok.at[0, h, 0, pl.ds(0, 7)], i_s.at[1, n, h])

    def gate_up(l, h, i):
        at, w = CHUNKS[i]
        value = tok[l, h].reshape(2 * 8 * ROWS, WIDTH)
        for n, weight in enumerate((wg, wu)):
            done = jnp.dot(value, weight[l, :, at : at + w], preferred_element_type=F32)
            part[h, :, :, :, 2 * at + n * w : 2 * at + n * w + w] = done.reshape(2, 8, ROWS, w)
        cols = pl.ds(2 * at, 2 * w)
        remote(part.at[h, 1 - c, :, :, cols], crecv.at[h, :, :, cols], c_s, (l, h, i), other_core)

    def scatter(l, h, i):
        at, w = CHUNKS[i]
        cols = pl.ds(2 * at, 2 * w)
        wait_bytes(crecv.at[h, :, :, cols], c_s.at[1, l, h, i])
        crecv[h, :, :, cols] = part[h, c, :, :, cols] + crecv[h, :, :, cols]
        rsend[l, h, :, :, cols] = crecv[h, :, :, cols].astype(BF16)
        for t, offset in enumerate(OFFSETS):
            to = chip_at(*offset)
            remote(rsend.at[l, h, to, :, cols], rrecv.at[l, h, t, :, cols], r_s, (l, h, i), (to * 2 + c, gy))

    def activate(l, h, i):
        at, w = CHUNKS[i]
        cols = pl.ds(2 * at, 2 * w)
        wait_bytes(rrecv.at[l, h, :, :, cols], r_s.at[1, l, h, i])
        total = crecv[h, chip, :, cols]
        for t in range(7):
            total = total + rrecv[l, h, t, :, cols].astype(F32)
        gate, up = total[:, :w], total[:, w:]
        hcols = pl.ds(at, w)
        hid[l, h, c, chip, :, hcols] = (gate / (1.0 + jnp.exp(-gate)) * up).astype(BF16)
        mine = hid.at[l, h, c, chip, :, hcols]
        for offset in OFFSETS:
            remote(mine, mine, a_s, (l, h, i), (chip_at(*offset) * 2 + c, gy))

    def forward(l, h, i):
        at, w = CHUNKS[i]
        hcols = pl.ds(at, w)
        wait_bytes(hid.at[l, h, 0, pl.ds(0, 7), :, hcols], a_s.at[1, l, h, i])
        rows = hid.at[l, h, c, :, :, hcols]
        remote(rows, rows, f_s, (l, h, i), other_core)

    def down(l, h, i):
        at, w = CHUNKS[i]
        hcols = pl.ds(at, w)
        wait_bytes(hid.at[l, h, 0, :, :, hcols], f_s.at[1, l, h, i])
        value = hid[l, h, :, :, :, hcols].reshape(2 * 8 * ROWS, w)
        done = jnp.dot(value, wd[l, at : at + w, :], preferred_element_type=F32).reshape(2, 8, ROWS, WIDTH)
        if i > 0:
            done = acc[h] + done
        acc[h] = done
        if i == NC - 1:
            zsend[l, h] = done.astype(BF16)
            for dz in range(1, 8):
                to = z_at(dz)
                remote(zsend.at[l, h, :, to], zrecv.at[l, h, dz - 1], z_s, (l, h), (gx, yh * 8 + to))

    def reduce_z(l, h):
        wait_bytes(zrecv.at[l, h], z_s.at[1, l, h])
        total = acc[h, :, z]
        for n in range(7):
            total = total + zrecv[l, h, n].astype(F32)
        ysum[l, h] = total
        if l == 0:
            remote(ysum.at[l, h], yrecv.at[l, h], y_s, (l, h), other_half)
        else:
            remote(ysum.at[l, h, 1 - yh], yrecv.at[l, h, 0], y_s, (l, h), other_half)

    def gather_z(h):
        wait_bytes(yrecv.at[0, h], y_s.at[1, 0, h])
        tok[1, h, :, z] = (ysum[0, h] + yrecv[0, h]).astype(BF16)
        mine = tok.at[1, h, :, z]
        for dz in range(1, 8):
            remote(mine, mine, t_s, (h,), (gx, yh * 8 + z_at(dz)))

    def gather_wait(h):
        wait_bytes(tok.at[1, h, :, pl.ds(0, 7)], t_s.at[1, h])

    def finish(h):
        wait_bytes(yrecv.at[1, h, 0], y_s.at[1, 1, h])
        out[pl.ds(ROWS * h, ROWS), :] = ysum[1, h, yh] + yrecv[1, h, 0]

    def send_core(l, h):
        for i in range(NC):
            at, w = CHUNKS[i]
            wait_bytes(crecv.at[h, :, :, pl.ds(2 * at, 2 * w)], c_s.at[0, l, h, i])

    first_send(0)
    first_send(1)
    first_forward(0)
    first_forward(1)
    for l in range(2):
        for h in range(HALVES):
            if l == 0:
                first_wait(h)
            else:
                gather_wait(h)
                send_core(0, h)
            if h == 0:
                wait_weight(3 * l)
                wait_weight(3 * l + 1)
            for i in range(NC):
                gate_up(l, h, i)
            for i in range(NC):
                scatter(l, h, i)
            if l == 1 and h == 0:
                reduce_z(0, 1)
                gather_z(1)
        wait_weight(3 * l + 2)
        for h in range(HALVES):
            activate(l, h, 0)
            for i in range(1, NC):
                activate(l, h, i)
                forward(l, h, i - 1)
            for i in range(NC):
                if i == 0:
                    forward(l, h, NC - 1)
                down(l, h, i)
        reduce_z(l, 0)
        if l == 0:
            gather_z(0)
    finish(0)
    reduce_z(1, 1)
    finish(1)

    for h in range(HALVES):
        block = tok.at[0, h, 0, 0]
        wait_bytes(block, i_s.at[0, 0, h])
        for n in (1, 2):
            wait_bytes(tok.at[0, h, 0, pl.ds(0, 7)], i_s.at[0, n, h])
        wait_bytes(tok.at[1, h, :, pl.ds(0, 7)], t_s.at[0, h])
        send_core(1, h)
        wait_bytes(yrecv.at[0, h], y_s.at[0, 0, h])
        wait_bytes(yrecv.at[1, h, 0], y_s.at[0, 1, h])
        for l in range(2):
            wait_bytes(zrecv.at[l, h], z_s.at[0, l, h])
            for i in range(NC):
                at, w = CHUNKS[i]
                hcols = pl.ds(at, w)
                wait_bytes(rrecv.at[l, h, :, :, pl.ds(2 * at, 2 * w)], r_s.at[0, l, h, i])
                wait_bytes(hid.at[l, h, 0, pl.ds(0, 7), :, hcols], a_s.at[0, l, h, i])
                wait_bytes(hid.at[l, h, 0, :, :, hcols], f_s.at[0, l, h, i])


def shards(*arrays):
    vmem = pl.BlockSpec(memory_space=pltpu.VMEM)
    anywhere = pl.BlockSpec(memory_space=pl.ANY)
    L, H = 2, HALVES
    sem = pltpu.SemaphoreType.DMA
    return pl.pallas_call(
        kernel,
        out_shape=jax.ShapeDtypeStruct((HALVES * ROWS, WIDTH), F32),
        in_specs=[vmem] + [anywhere] * 6,
        out_specs=vmem,
        scratch_shapes=[
            pltpu.VMEM((L, WIDTH, HIDDEN), BF16),
            pltpu.VMEM((L, WIDTH, HIDDEN), BF16),
            pltpu.VMEM((L, HIDDEN, WIDTH), BF16),
            pltpu.VMEM((L, H, 2, 8, ROWS, WIDTH), BF16),
            pltpu.VMEM((H, 2, 8, ROWS, 2 * HIDDEN), F32),
            pltpu.VMEM((H, 8, ROWS, 2 * HIDDEN), F32),
            pltpu.VMEM((L, H, 8, ROWS, 2 * HIDDEN), BF16),
            pltpu.VMEM((L, H, 7, ROWS, 2 * HIDDEN), BF16),
            pltpu.VMEM((L, H, 2, 8, ROWS, HIDDEN), BF16),
            pltpu.VMEM((H, 2, 8, ROWS, WIDTH), F32),
            pltpu.VMEM((L, H, 2, 8, ROWS, WIDTH), BF16),
            pltpu.VMEM((L, H, 7, 2, ROWS, WIDTH), BF16),
            pltpu.VMEM((L, H, 2, ROWS, WIDTH), F32),
            pltpu.VMEM((L, H, 2, ROWS, WIDTH), F32),
            sem((6,)),
            sem((2, L, H, NC)),
            sem((2, L, H, NC)),
            sem((2, L, H, NC)),
            sem((2, L, H, NC)),
            sem((2, L, H)),
            sem((2, L, H)),
            sem((2, H)),
            sem((2, 3, H)),
        ],
        compiler_params=pltpu.CompilerParams(has_side_effects=True, vmem_limit_bytes=56 * 2**20),
        cost_estimate=pl.CostEstimate(flops=6 * 2 * 512 * 512 * 1792, bytes_accessed=6 * 512 * 1792 * 2, transcendentals=0),
    )(*arrays)


def solution(mesh):
    in_specs = (
        P("gy", "gx"),
        P("gx", "gy"),
        P("gx", "gy"),
        P("gy", "gx"),
        P("gx", "gy"),
        P("gx", "gy"),
        P("gy", "gx"),
    )
    return jax.shard_map(shards, mesh=mesh, in_specs=in_specs, out_specs=P("gy", "gx"), check_vma=False)
```

time: 774 us -> 165 us (0.21)
  waiting for transfers between devices: 653 us -> 0 us
  Pallas kernels: 0 us -> 164 us
  blocking collectives: 75.4 us -> 0 us
  matrix products: 14.4 us -> 0 us
  between operations: 13.5 us -> 0.01 us
  other arithmetic: 12.4 us -> 0 us
    reduce_scatter x4 -> x0, waiting for transfers between devices: 577 us -> none  [the longest x2 391 us: shards(): lax.psum_scatter(partial_value, 'gy', scatter_dimension=0, tiled=True)]
    pallas_call x0 -> x1, Pallas kernels: none -> 164 us  [shards(): pl.pallas_call(kernel, out_shape=jax.ShapeDtypeStruct((HALVES * ROWS, WID...]
    all_gather x2 -> x0, waiting for transfers between devices: 76.2 us -> none  [down_partial(): lax.all_gather(hidden, 'gx', axis=0, tiled=True)]
    all_gather x2 -> x0, blocking collectives: 75.4 us -> none  [the longest x1 41 us: shards(): gathered = lax.all_gather(tokens, 'gy', axis=0, tiled=True)]
    dot_general x6 -> x0, matrix products: 14.4 us -> none  [the longest x2 8.28 us: down_partial(): jnp.dot(lax.all_gather(hidden, 'gx', axis=0, tiled=True), down_weight, pr...]
    concatenate x2 -> x0, other arithmetic: 8.03 us -> none  [hidden_units(): jnp.concatenate([gate_part, up_part], axis=1)]
  transfers between devices with their start and end apart: 6 -> 0, of which waited for: 6 -> 0; matrix products, arithmetic and copies ran while one was open for 0% -> 0% of each run, Pallas kernels for 0% -> 0%
where the time goes in v1:
time: 165 us
  Pallas kernels  164 us (99%)
    pallas_call x1, Pallas kernels, shards(): pl.pallas_call(kernel, out_shape=jax.ShapeDtypeStruct((HALVES * ROWS, WID...  164 us

profile of v1, /device:TPU:1, one launch (start us, length us, event | category | flops | bytes accessed | tf_op | source)
XLA Modules:
  0.0 165.0 jit_solution(10956648722256897593)
XLA Ops:
  0.0 163.5 %shard_map.73 = f32[32,512]{1,0:T(8,128)} custom-call(bf16[32,512]{1,0:T(8,128)(2,1)} %tokens.1, bf16[512,1792]{1,0:T(8,128)(2,1)} %g0.1, bf16[512,1792]{1,0:T(8,128)(2,1)} %u0.1, bf16[1792,512]{1,0:T(8,128)(2,1)} %d0.1, bf16[512,1792]{1,0:T(8,128)(2,1)} %g1.1, bf16[512,1792]{1,0:T(8,128)(2,1)} %u1_.1, bf16[1792,512]{1,0:T(8,128)(2,1)} %d1.1), custom_call_target="tpu_custom_call" | custom-call | flops 5637144576 | bytes 11010048 | tf_op jit(solution)/shard_map/pallas_call | solution.py:223
  163.5 1.5 copy.9

commit v2 on v1

--- a/solution.py
+++ b/solution.py
@@ -47,6 +47,13 @@
     def z_at(dz):
         return lax.rem(z + dz, 8)
 
+    partners = [other_core, other_half]
+    partners += [(chip_at(*offset) * 2 + c, gy) for offset in OFFSETS]
+    partners += [(gx, yh * 8 + z_at(dz)) for dz in range(1, 8)]
+    barrier = pltpu.get_barrier_semaphore()
+    for device in partners:
+        pl.semaphore_signal(barrier, inc=1, device_id=device, device_id_type=pl.DeviceIdType.MESH)
+
     for n, (src, dst) in enumerate(
         ((g0, wg.at[0]), (u0, wu.at[0]), (d0, wd.at[0]), (g1, wg.at[1]), (u1, wu.at[1]), (d1, wd.at[1]))
     ):
@@ -55,6 +62,8 @@
     def wait_weight(n):
         ref = (wg, wu, wd)[n % 3].at[n // 3]
         wait_bytes(ref, w_s.at[n])
+
+    pl.semaphore_wait(barrier, len(partners))
 
     def first_send(h):
         tok[0, h, yh, z] = tokens[pl.ds(ROWS * h, ROWS), :]
@@ -158,10 +167,9 @@
             at, w = CHUNKS[i]
             wait_bytes(crecv.at[h, :, :, pl.ds(2 * at, 2 * w)], c_s.at[0, l, h, i])
 
-    first_send(0)
-    first_send(1)
-    first_forward(0)
-    first_forward(1)
+    for h in range(HALVES):
+        first_send(h)
+        first_forward(h)
     for l in range(2):
         for h in range(HALVES):
             if l == 0:
@@ -176,24 +184,20 @@
                 gate_up(l, h, i)
             for i in range(NC):
                 scatter(l, h, i)
-            if l == 1 and h == 0:
-                reduce_z(0, 1)
-                gather_z(1)
         wait_weight(3 * l + 2)
         for h in range(HALVES):
-            activate(l, h, 0)
-            for i in range(1, NC):
+            for i in range(NC):
                 activate(l, h, i)
-                forward(l, h, i - 1)
-            for i in range(NC):
-                if i == 0:
-                    forward(l, h, NC - 1)
+        for h in range(HALVES):
+            for i in range(NC):
+                forward(l, h, i)
+            for i in range(NC):
                 down(l, h, i)
-        reduce_z(l, 0)
-        if l == 0:
-            gather_z(0)
+        for h in range(HALVES):
+            reduce_z(l, h)
+            if l == 0:
+                gather_z(h)
     finish(0)
-    reduce_z(1, 1)
     finish(1)
 
     for h in range(HALVES):
@@ -250,7 +254,7 @@
             sem((2, H)),
             sem((2, 3, H)),
         ],
-        compiler_params=pltpu.CompilerParams(has_side_effects=True, vmem_limit_bytes=56 * 2**20),
+        compiler_params=pltpu.CompilerParams(collective_id=0, has_side_effects=True, vmem_limit_bytes=56 * 2**20),
         cost_estimate=pl.CostEstimate(flops=6 * 2 * 512 * 512 * 1792, bytes_accessed=6 * 512 * 1792 * 2, transcendentals=0),
     )(*arrays)
 

time: 165 us -> 130 us (0.79)
  Pallas kernels: 164 us -> 127 us
    pallas_call x1, Pallas kernels: 164 us -> 127 us  [shards(): pl.pallas_call(kernel, out_shape=jax.ShapeDtypeStruct((HALVES * ROWS, WID...]
where the time goes in v2:
time: 130 us; the launch traced here: 129 us
  Pallas kernels  127 us (98%)
  local copies, waits for them, and re-layouts  1.47 us (1%)
    pallas_call x1, Pallas kernels, shards(): pl.pallas_call(kernel, out_shape=jax.ShapeDtypeStruct((HALVES * ROWS, WID...  127 us

profile of v2, /device:TPU:1, one launch (start us, length us, event | category | flops | bytes accessed | tf_op | source)
XLA Modules:
  0.0 128.8 jit_solution(16533649165432681303)
XLA Ops:
  0.0 127.4 %shard_map.73 = f32[32,512]{1,0:T(8,128)} custom-call(bf16[32,512]{1,0:T(8,128)(2,1)} %tokens.1, bf16[512,1792]{1,0:T(8,128)(2,1)} %g0.1, bf16[512,1792]{1,0:T(8,128)(2,1)} %u0.1, bf16[1792,512]{1,0:T(8,128)(2,1)} %d0.1, bf16[512,1792]{1,0:T(8,128)(2,1)} %g1.1, bf16[512,1792]{1,0:T(8,128)(2,1)} %u1_.1, bf16[1792,512]{1,0:T(8,128)(2,1)} %d1.1), custom_call_target="tpu_custom_call" | custom-call | flops 5637144576 | bytes 11010048 | tf_op jit(solution)/shard_map/pallas_call | solution.py:227
  127.4 1.5 %copy.9 = f32[32,512]{1,0:T(8,128)} copy(f32[32,512]{1,0:T(8,128)} %shard_map.73) | data formatting | bytes 131072

commit v3 on v0

v3 whole, which is shorter than its diff:
```python
import jax
import jax.numpy as jnp
from jax import lax
from jax.experimental import pallas as pl
from jax.experimental.pallas import tpu as pltpu
from jax.sharding import PartitionSpec as P

PARTS = tuple((h, q) for h in range(2) for q in range(2))
ROWS = 16
WIDTH = 512
HALF = 896
OFFSETS = tuple((dx, dy) for dx in range(4) for dy in range(2) if dx + dy > 0)
BF16 = jnp.bfloat16
F32 = jnp.float32
ORDER = (
    ("gate_up", 0, 0), ("gate_up", 0, 1), ("scatter0", 0, 0), ("scatter1", 0, 0),
    ("gate_up", 0, 2), ("scatter0", 0, 1), ("gate_up", 0, 3), ("scatter1", 0, 1),
    ("scatter0", 0, 2), ("middle0", 0, 0), ("middle1", 0, 0), ("scatter1", 0, 2),
    ("scatter0", 0, 3), ("middle0", 0, 1), ("scatter1", 0, 3), ("middle1", 0, 1),
    ("middle0", 0, 2), ("activate", 0, 0), ("middle1", 0, 2), ("middle0", 0, 3),
    ("activate", 0, 1), ("middle1", 0, 3), ("activate", 0, 2), ("forward", 0, 0),
    ("down", 0, 0), ("forward", 0, 1), ("activate", 0, 3), ("down", 0, 1),
    ("forward", 0, 2), ("down", 0, 2), ("reduce_z", 0, 0), ("forward", 0, 3),
    ("down", 0, 3), ("reduce_z", 0, 1), ("gather_z", 0, 0), ("reduce_z", 0, 2),
    ("gather_z", 0, 1), ("reduce_z", 0, 3), ("gather_z", 0, 2), ("gate_up", 1, 0),
    ("gather_z", 0, 3), ("scatter0", 1, 0), ("gate_up", 1, 1), ("scatter1", 1, 0),
    ("gate_up", 1, 2), ("scatter1", 1, 1), ("scatter0", 1, 1), ("middle0", 1, 0),
    ("gate_up", 1, 3), ("middle1", 1, 0), ("scatter1", 1, 2), ("scatter0", 1, 2),
    ("scatter0", 1, 3), ("middle1", 1, 1), ("scatter1", 1, 3), ("middle0", 1, 1),
    ("activate", 1, 0), ("middle1", 1, 2), ("middle0", 1, 2), ("middle1", 1, 3),
    ("middle0", 1, 3), ("activate", 1, 1), ("forward", 1, 0), ("activate", 1, 2),
    ("down", 1, 0), ("activate", 1, 3), ("forward", 1, 1), ("down", 1, 1),
    ("forward", 1, 2), ("down", 1, 2), ("reduce_z", 1, 0), ("forward", 1, 3),
    ("down", 1, 3), ("gather_z", 1, 0), ("reduce_z", 1, 1), ("reduce_z", 1, 2),
    ("gather_z", 1, 1), ("reduce_z", 1, 3), ("gather_z", 1, 2), ("gather_z", 1, 3),
)


def wait_bytes(ref, sem):
    pltpu.make_async_copy(ref, ref, sem).wait()


def kernel(
    tokens, g0, u0, d0, g1, u1, d1, out,
    wgu, wd, tok, pown, pother, crecv, xsend, xrecv, ysend, yback, msend, mrecv, nsend, nrecv, mown, hid, acc, zsend, zrecv, ysum, yrecv,
    w_s, c_s, r_s, m_s, a_s, f_s, z_s, y_s, t_s, i_s,
):
    gx, gy = lax.axis_index("gx"), lax.axis_index("gy")
    c, chip = lax.rem(gx, 2), gx // 2
    yl, x = lax.rem(chip, 2), chip // 2
    z, yh = lax.rem(gy, 8), gy // 8

    def remote(src, dst, sems, index, device):
        pltpu.make_async_remote_copy(
            src_ref=src, dst_ref=dst, send_sem=sems.at[(0, *index)], recv_sem=sems.at[(1, *index)],
            device_id=device, device_id_type=pl.DeviceIdType.MESH,
        ).start()

    other_core = (chip * 2 + 1 - c, gy)
    other_half = (gx, (1 - yh) * 8 + z)
    other_y = ((x * 2 + 1 - yl) * 2 + c, gy)

    def chip_at(dx, dy):
        return lax.rem(x + dx, 4) * 2 + lax.rem(yl + dy, 2)

    def z_at(dz):
        return lax.rem(z + dz, 8)

    partners = [other_core, other_half]
    partners += [(chip_at(*offset) * 2 + c, gy) for offset in OFFSETS]
    partners += [(gx, yh * 8 + z_at(dz)) for dz in range(1, 8)]
    barrier = pltpu.get_barrier_semaphore()
    for device in partners:
        pl.semaphore_signal(barrier, inc=1, device_id=device, device_id_type=pl.DeviceIdType.MESH)

    weights = ((g0, u0, d0), (g1, u1, d1))
    halves = [pl.ds(k * HALF, HALF) for k in range(2)]

    def weight_copies(l):
        gate, up, down = weights[l]
        for k in range(2):
            for n, weight in enumerate((gate, up)):
                pltpu.make_async_copy(weight.at[:, halves[k]], wgu.at[l, k, n], w_s.at[l, 0, k, n]).start()
        for k in range(2):
            pltpu.make_async_copy(down.at[halves[k], :], wd.at[l, k], w_s.at[l, 1, k, 0]).start()

    weight_copies(0)
    weight_copies(1)
    for h in range(2):
        tok[0, h, yh, z] = tokens[pl.ds(ROWS * h, ROWS), :]
    pl.semaphore_wait(barrier, len(partners))

    def first_send(h):
        mine = tok.at[0, h, yh, z]
        remote(mine, mine, i_s, (0, h), other_half)

    def first_own(h):
        mine = tok.at[0, h, yh, z]
        for dz in range(1, 8):
            remote(mine, mine, i_s, (1, h), (gx, yh * 8 + z_at(dz)))

    def first_forward(h):
        theirs = tok.at[0, h, 1 - yh, z]
        wait_bytes(theirs, i_s.at[1, 0, h])
        for dz in range(1, 8):
            remote(theirs, theirs, i_s, (2, h), (gx, yh * 8 + z_at(dz)))

    def gate_up(l, s):
        h, q = PARTS[s]
        if l == 0:
            if q == 0:
                for n in (1, 2):
                    wait_bytes(tok.at[0, h, 0, pl.ds(0, 7)], i_s.at[1, n, h])
        else:
            wait_bytes(tok.at[1, h, q, pl.ds(0, 7)], t_s.at[1, s])
            for n in range(2):
                wait_bytes(crecv.at[s, n], c_s.at[0, 0, s, n])
        if s == 0:
            for k in range(2):
                for n in range(2):
                    wait_bytes(wgu.at[l, k, n], w_s.at[l, 0, k, n])
        value = tok[l, h, q].reshape(8 * ROWS, WIDTH)
        for n in range(2):
            done = jnp.dot(value, wgu[l, 1 - c, n], preferred_element_type=F32)
            pother[s, n] = done.reshape(4, 2, ROWS, HALF)
            remote(pother.at[s, n], crecv.at[s, n], c_s, (l, s, n), other_core)
        for n in range(2):
            done = jnp.dot(value, wgu[l, c, n], preferred_element_type=F32)
            pown[s, n] = done.reshape(4, 2, ROWS, HALF)

    def scatter(l, s, n):
        wait_bytes(crecv.at[s, n], c_s.at[1, l, s, n])
        if n == 0:
            xsend[l, s] = (pown[s, 0] + crecv[s, 0]).astype(BF16)
            for dx in range(1, 4):
                to = lax.rem(x + dx, 4)
                remote(xsend.at[l, s, to], xrecv.at[l, s, dx - 1], r_s, (l, s, 0), ((to * 2 + yl) * 2 + c, gy))
        else:
            ysend[l, s] = (pown[s, 1, :, 1 - yl] + crecv[s, 1, :, 1 - yl]).astype(BF16)
            remote(ysend.at[l, s], yback.at[l, s], r_s, (l, s, 1), other_y)

    def middle(l, s, n):
        if n == 0:
            wait_bytes(xrecv.at[l, s], r_s.at[1, l, s, 0])
            for side in (1 - yl, yl):
                total = pown[s, 0, x, side] + crecv[s, 0, x, side]
                for t in range(3):
                    total = total + xrecv[l, s, t, side].astype(F32)
                if side is yl:
                    mown[s, 0] = total
                else:
                    msend[l, s] = total.astype(BF16)
                    remote(msend.at[l, s], mrecv.at[l, s], m_s, (l, s, 0), other_y)
        else:
            wait_bytes(yback.at[l, s], r_s.at[1, l, s, 1])
            nsend[l, s] = (pown[s, 1, :, yl] + crecv[s, 1, :, yl] + yback[l, s].astype(F32)).astype(BF16)
            for dx in range(1, 4):
                to = lax.rem(x + dx, 4)
                remote(nsend.at[l, s, to], nrecv.at[l, s, dx - 1], m_s, (l, s, 1), ((to * 2 + yl) * 2 + c, gy))
            mown[s, 1] = pown[s, 1, x, yl] + crecv[s, 1, x, yl] + yback[l, s, x].astype(F32)

    def activate(l, s):
        wait_bytes(mrecv.at[l, s], m_s.at[1, l, s, 0])
        gate = mown[s, 0] + mrecv[l, s].astype(F32)
        wait_bytes(nrecv.at[l, s], m_s.at[1, l, s, 1])
        up = mown[s, 1]
        for t in range(3):
            up = up + nrecv[l, s, t].astype(F32)
        hid[l, s, c, chip] = (gate / (1.0 + jnp.exp(-gate)) * up).astype(BF16)
        mine = hid.at[l, s, c, chip]
        for offset in OFFSETS:
            remote(mine, mine, a_s, (l, s), (chip_at(*offset) * 2 + c, gy))

    def half_down(l, s, k):
        value = hid[l, s, k].reshape(8 * ROWS, HALF)
        return jnp.dot(value, wd[l, k], preferred_element_type=F32).reshape(8, ROWS, WIDTH)

    def forward(l, s):
        wait_bytes(hid.at[l, s, 0, pl.ds(0, 7)], a_s.at[1, l, s])
        rows = hid.at[l, s, c]
        remote(rows, rows, f_s, (l, s), other_core)
        if s == 0:
            for k in range(2):
                wait_bytes(wd.at[l, k], w_s.at[l, 1, k, 0])
        acc[s] = half_down(l, s, c)

    def down(l, s):
        wait_bytes(hid.at[l, s, 0], f_s.at[1, l, s])
        done = acc[s] + half_down(l, s, 1 - c)
        acc[s] = done
        zsend[l, s] = done.astype(BF16)
        for dz in range(1, 8):
            to = z_at(dz)
            remote(zsend.at[l, s, to], zrecv.at[l, s, dz - 1], z_s, (l, s), (gx, yh * 8 + to))

    def reduce_z(l, s):
        wait_bytes(zrecv.at[l, s], z_s.at[1, l, s])
        total = acc[s, z]
        for n in range(7):
            total = total + zrecv[l, s, n].astype(F32)
        ysum[l, s] = total
        remote(ysum.at[l, s], yrecv.at[l, s], y_s, (l, s), other_half)

    def gather_z(l, s):
        h, q = PARTS[s]
        wait_bytes(yrecv.at[l, s], y_s.at[1, l, s])
        total = ysum[l, s] + yrecv[l, s]
        if l == 0:
            tok[1, h, q, z] = total.astype(BF16)
            mine = tok.at[1, h, q, z]
            for dz in range(1, 8):
                remote(mine, mine, t_s, (s,), (gx, yh * 8 + z_at(dz)))
        else:

            @pl.when(yh == q)
            def _():
                out[pl.ds(ROWS * h, ROWS), :] = total

    steps = {
        "gate_up": gate_up,
        "scatter0": lambda l, s: scatter(l, s, 0),
        "scatter1": lambda l, s: scatter(l, s, 1),
        "middle0": lambda l, s: middle(l, s, 0),
        "middle1": lambda l, s: middle(l, s, 1),
        "activate": activate,
        "forward": forward,
        "down": down,
        "reduce_z": reduce_z,
        "gather_z": gather_z,
    }
    first_send(0)
    first_own(0)
    first_send(1)
    first_forward(0)
    first_own(1)
    first_forward(1)
    for name, l, s in ORDER:
        steps[name](l, s)

    for h in range(2):
        wait_bytes(tok.at[0, h, 0, 0], i_s.at[0, 0, h])
        for n in (1, 2):
            wait_bytes(tok.at[0, h, 0, pl.ds(0, 7)], i_s.at[0, n, h])
    for s in range(4):
        h, q = PARTS[s]
        wait_bytes(tok.at[1, h, q, pl.ds(0, 7)], t_s.at[0, s])
        for l in range(2):
            for n in range(2):
                if l == 1:
                    wait_bytes(crecv.at[s, n], c_s.at[0, l, s, n])
                wait_bytes((xrecv, yback)[n].at[l, s], r_s.at[0, l, s, n])
                wait_bytes((mrecv, nrecv)[n].at[l, s], m_s.at[0, l, s, n])
            wait_bytes(hid.at[l, s, 0, pl.ds(0, 7)], a_s.at[0, l, s])
            wait_bytes(hid.at[l, s, 0], f_s.at[0, l, s])
            wait_bytes(zrecv.at[l, s], z_s.at[0, l, s])
            wait_bytes(yrecv.at[l, s], y_s.at[0, l, s])


def shards(*arrays):
    vmem = pl.BlockSpec(memory_space=pltpu.VMEM)
    anywhere = pl.BlockSpec(memory_space=pl.ANY)
    L, S = 2, len(PARTS)
    sem = pltpu.SemaphoreType.DMA
    return pl.pallas_call(
        kernel,
        out_shape=jax.ShapeDtypeStruct((2 * ROWS, WIDTH), F32),
        in_specs=[vmem] + [anywhere] * 6,
        out_specs=vmem,
        scratch_shapes=[
            pltpu.VMEM((L, 2, 2, WIDTH, HALF), BF16),
            pltpu.VMEM((L, 2, HALF, WIDTH), BF16),
            pltpu.VMEM((L, 2, 2, 8, ROWS, WIDTH), BF16),
            pltpu.VMEM((S, 2, 4, 2, ROWS, HALF), F32),
            pltpu.VMEM((S, 2, 4, 2, ROWS, HALF), F32),
            pltpu.VMEM((S, 2, 4, 2, ROWS, HALF), F32),
            pltpu.VMEM((L, S, 4, 2, ROWS, HALF), BF16),
            pltpu.VMEM((L, S, 3, 2, ROWS, HALF), BF16),
            pltpu.VMEM((L, S, 4, ROWS, HALF), BF16),
            pltpu.VMEM((L, S, 4, ROWS, HALF), BF16),
            pltpu.VMEM((L, S, ROWS, HALF), BF16),
            pltpu.VMEM((L, S, ROWS, HALF), BF16),
            pltpu.VMEM((L, S, 4, ROWS, HALF), BF16),
            pltpu.VMEM((L, S, 3, ROWS, HALF), BF16),
            pltpu.VMEM((S, 2, ROWS, HALF), F32),
            pltpu.VMEM((L, S, 2, 8, ROWS, HALF), BF16),
            pltpu.VMEM((S, 8, ROWS, WIDTH), F32),
            pltpu.VMEM((L, S, 8, ROWS, WIDTH), BF16),
            pltpu.VMEM((L, S, 7, ROWS, WIDTH), BF16),
            pltpu.VMEM((L, S, ROWS, WIDTH), F32),
            pltpu.VMEM((L, S, ROWS, WIDTH), F32),
            sem((L, 2, 2, 2)),
            sem((2, L, S, 2)),
            sem((2, L, S, 2)),
            sem((2, L, S, 2)),
            sem((2, L, S)),
            sem((2, L, S)),
            sem((2, L, S)),
            sem((2, L, S)),
            sem((2, S)),
            sem((2, 3, 2)),
        ],
        compiler_params=pltpu.CompilerParams(collective_id=0, has_side_effects=True, vmem_limit_bytes=56 * 2**20),
        cost_estimate=pl.CostEstimate(flops=6 * 2 * 512 * 512 * 1792, bytes_accessed=6 * 512 * 1792 * 2, transcendentals=0),
    )(*arrays)


def solution(mesh):
    weights = (P("gx", "gy"), P("gx", "gy"), P("gy", "gx"))
    in_specs = (P("gy", "gx"), *weights, *weights)
    return jax.shard_map(shards, mesh=mesh, in_specs=in_specs, out_specs=P("gy", "gx"), check_vma=False)
```

time: 774 us -> 111 us (0.14)
  waiting for transfers between devices: 653 us -> 0 us
  Pallas kernels: 0 us -> 109 us
  blocking collectives: 75.4 us -> 0 us
  matrix products: 14.4 us -> 0 us
  between operations: 13.5 us -> 0.01 us
  other arithmetic: 12.4 us -> 0 us
    reduce_scatter x4 -> x0, waiting for transfers between devices: 577 us -> none  [the longest x2 391 us: shards(): lax.psum_scatter(partial_value, 'gy', scatter_dimension=0, tiled=True)]
    pallas_call x0 -> x1, Pallas kernels: none -> 109 us  [shards(): pl.pallas_call(kernel, out_shape=jax.ShapeDtypeStruct((2 * ROWS, WIDTH),...]
    all_gather x2 -> x0, waiting for transfers between devices: 76.2 us -> none  [down_partial(): lax.all_gather(hidden, 'gx', axis=0, tiled=True)]
    all_gather x2 -> x0, blocking collectives: 75.4 us -> none  [the longest x1 41 us: shards(): gathered = lax.all_gather(tokens, 'gy', axis=0, tiled=True)]
    dot_general x6 -> x0, matrix products: 14.4 us -> none  [the longest x2 8.28 us: down_partial(): jnp.dot(lax.all_gather(hidden, 'gx', axis=0, tiled=True), down_weight, pr...]
    concatenate x2 -> x0, other arithmetic: 8.03 us -> none  [hidden_units(): jnp.concatenate([gate_part, up_part], axis=1)]
  transfers between devices with their start and end apart: 6 -> 0, of which waited for: 6 -> 0; matrix products, arithmetic and copies ran while one was open for 0% -> 0% of each run, Pallas kernels for 0% -> 0%
where the time goes in v3:
time: 111 us
  Pallas kernels  109 us (98%)
  local copies, waits for them, and re-layouts  1.47 us (1%)
    pallas_call x1, Pallas kernels, shards(): pl.pallas_call(kernel, out_shape=jax.ShapeDtypeStruct((2 * ROWS, WIDTH),...  109 us

profile of v3, /device:TPU:1, one launch (start us, length us, event | category | flops | bytes accessed | tf_op | source)
XLA Modules:
  0.0 110.6 jit_solution(5293834520719255458)
XLA Ops:
  0.0 109.1 %shard_map.73 = f32[32,512]{1,0:T(8,128)} custom-call(bf16[32,512]{1,0:T(8,128)(2,1)} %tokens.1, bf16[512,1792]{1,0:T(8,128)(2,1)} %g0.1, bf16[512,1792]{1,0:T(8,128)(2,1)} %u0.1, bf16[1792,512]{1,0:T(8,128)(2,1)} %d0.1, bf16[512,1792]{1,0:T(8,128)(2,1)} %g1.1, bf16[512,1792]{1,0:T(8,128)(2,1)} %u1_.1, bf16[1792,512]{1,0:T(8,128)(2,1)} %d1.1), custom_call_target="tpu_custom_call" | custom-call | flops 5637144576 | bytes 11010048 | tf_op jit(solution)/shard_map/pallas_call | solution.py:264
  109.1 1.5 %copy.9 = f32[32,512]{1,0:T(8,128)} copy(f32[32,512]{1,0:T(8,128)} %shard_map.73) | data formatting | bytes 131072

commit v4 on v3

v4 whole, which is shorter than its diff:
```python
import jax
import jax.numpy as jnp
from jax import lax
from jax.experimental import pallas as pl
from jax.experimental.pallas import tpu as pltpu
from jax.sharding import PartitionSpec as P

PARTS = tuple((h, q) for h in range(2) for q in range(2))
ROWS = 16
WIDTH = 512
HALF = 896
OFFSETS = ((2, 1), (1, 1), (3, 1), (2, 0), (1, 0), (3, 0), (0, 1))
ALONG_X = (2, 1, 3)
ALONG_Z = (4, 3, 5, 2, 6, 1, 7)
BF16 = jnp.bfloat16
F32 = jnp.float32
ORDER = (
    ("gate_up", 0, 0), ("gate_up", 0, 1), ("scatter1", 0, 0), ("scatter0", 0, 0),
    ("gate_up", 0, 2), ("up0", 0, 0), ("scatter1", 0, 1), ("scatter0", 0, 1),
    ("up1", 0, 0), ("gate0", 0, 0), ("gate1", 0, 0), ("scatter0", 0, 2),
    ("up0", 0, 1), ("scatter1", 0, 2), ("up1", 0, 1), ("gate_up", 0, 3),
    ("activate", 0, 0), ("gate1", 0, 1), ("gate0", 0, 1), ("gate1", 0, 2),
    ("up1", 0, 2), ("scatter1", 0, 3), ("up0", 0, 2), ("scatter0", 0, 3),
    ("gate0", 0, 2), ("activate", 0, 1), ("forward", 0, 0), ("down", 0, 0),
    ("up1", 0, 3), ("activate", 0, 2), ("gate1", 0, 3), ("up0", 0, 3),
    ("gate0", 0, 3), ("forward", 0, 1), ("down", 0, 1), ("reduce_z", 0, 0),
    ("forward", 0, 2), ("activate", 0, 3), ("down", 0, 2), ("gather_z", 0, 0),
    ("forward", 0, 3), ("reduce_z", 0, 1), ("down", 0, 3), ("reduce_z", 0, 2),
    ("gather_z", 0, 1), ("gate_up", 1, 0), ("gather_z", 0, 2), ("scatter1", 1, 0),
    ("scatter0", 1, 0), ("reduce_z", 0, 3), ("up0", 1, 0), ("gate_up", 1, 1),
    ("up1", 1, 0), ("gate0", 1, 0), ("scatter1", 1, 1), ("gather_z", 0, 3),
    ("gate1", 1, 0), ("scatter0", 1, 1), ("gate_up", 1, 2), ("activate", 1, 0),
    ("scatter1", 1, 2), ("gate0", 1, 1), ("scatter0", 1, 2), ("up1", 1, 1),
    ("gate_up", 1, 3), ("up0", 1, 1), ("up0", 1, 2), ("gate1", 1, 1),
    ("scatter0", 1, 3), ("scatter1", 1, 3), ("gate0", 1, 2), ("up1", 1, 2),
    ("activate", 1, 1), ("up0", 1, 3), ("up1", 1, 3), ("gate1", 1, 2),
    ("gate0", 1, 3), ("forward", 1, 0), ("activate", 1, 2), ("gate1", 1, 3),
    ("down", 1, 0), ("activate", 1, 3), ("forward", 1, 1), ("down", 1, 1),
    ("forward", 1, 2), ("down", 1, 2), ("forward", 1, 3), ("reduce_z", 1, 0),
    ("down", 1, 3), ("reduce_z", 1, 1), ("gather_z", 1, 0), ("reduce_z", 1, 2),
    ("reduce_z", 1, 3), ("gather_z", 1, 1), ("gather_z", 1, 2), ("gather_z", 1, 3),
)


def wait_bytes(ref, sem):
    pltpu.make_async_copy(ref, ref, sem).wait()


def kernel(
    tokens, g0, u0, d0, g1, u1, d1, out,
    wgu, wd, tok, pown, pother, crecv, pother2, crecv2, xsend, xrecv, ysend, yback, msend, mrecv, nsend, nrecv, mown, hid, acc, zsend, zrecv, ysum, yrecv,
    w_s, c_s, r_s, m_s, a_s, f_s, z_s, y_s, t_s, i_s,
):
    gx, gy = lax.axis_index("gx"), lax.axis_index("gy")
    c, chip = lax.rem(gx, 2), gx // 2
    yl, x = lax.rem(chip, 2), chip // 2
    z, yh = lax.rem(gy, 8), gy // 8

    def remote(src, dst, sems, index, device):
        pltpu.make_async_remote_copy(
            src_ref=src, dst_ref=dst, send_sem=sems.at[(0, *index)], recv_sem=sems.at[(1, *index)],
            device_id=device, device_id_type=pl.DeviceIdType.MESH,
        ).start()

    other_core = (chip * 2 + 1 - c, gy)
    other_half = (gx, (1 - yh) * 8 + z)
    other_y = ((x * 2 + 1 - yl) * 2 + c, gy)

    x_at = [lax.rem(x + dx, 4) for dx in range(4)]
    x_device = [((to * 2 + yl) * 2 + c, gy) for to in x_at]
    chip_device = [((x_at[dx] * 2 + lax.rem(yl + dy, 2)) * 2 + c, gy) for dx, dy in OFFSETS]
    z_at = [lax.rem(z + dz, 8) for dz in range(8)]
    z_device = [(gx, yh * 8 + to) for to in z_at]
    partners = [z_device[dz] for dz in ALONG_Z] + [other_half] + chip_device + [other_core]
    barrier = pltpu.get_barrier_semaphore()
    for device in partners:
        pl.semaphore_signal(barrier, inc=1, device_id=device, device_id_type=pl.DeviceIdType.MESH)

    weights = ((g0, u0, d0), (g1, u1, d1))
    halves = [pl.ds(k * HALF, HALF) for k in range(2)]

    def weight_copies(l):
        gate, up, down = weights[l]
        for k in range(2):
            for n, weight in enumerate((gate, up)):
                pltpu.make_async_copy(weight.at[:, halves[k]], wgu.at[l, k, n], w_s.at[l, 0, k, n]).start()
        for k in range(2):
            pltpu.make_async_copy(down.at[halves[k], :], wd.at[l, k], w_s.at[l, 1, k, 0]).start()

    weight_copies(0)
    weight_copies(1)
    for h in range(2):
        tok[0, h, yh, z] = tokens[pl.ds(ROWS * h, ROWS), :]
    pl.semaphore_wait(barrier, len(partners))

    def first_send(h):
        mine = tok.at[0, h, yh, z]
        remote(mine, mine, i_s, (0, h), other_half)

    def first_own(h):
        mine = tok.at[0, h, yh, z]
        for dz in ALONG_Z:
            remote(mine, mine, i_s, (1, h), z_device[dz])

    def first_forward(h):
        theirs = tok.at[0, h, 1 - yh, z]
        wait_bytes(theirs, i_s.at[1, 0, h])
        for dz in ALONG_Z:
            remote(theirs, theirs, i_s, (2, h), z_device[dz])

    core_buffers = ((pother, crecv), (pother2, crecv2))

    def gate_up(l, s):
        h, q = PARTS[s]
        if l == 0:
            if q == 0:
                for n in (1, 2):
                    wait_bytes(tok.at[0, h, 0, pl.ds(0, 7)], i_s.at[1, n, h])
        else:
            wait_bytes(tok.at[1, h, q, pl.ds(0, 7)], t_s.at[1, s])
            for n in range(2):
                wait_bytes(crecv.at[s, n], c_s.at[0, 0, s, n])
        sent, landed = core_buffers[l]
        if s == 0:
            for k in range(2):
                for n in range(2):
                    wait_bytes(wgu.at[l, k, n], w_s.at[l, 0, k, n])
        value = tok[l, h, q].reshape(8 * ROWS, WIDTH)
        for n in (1, 0):
            done = jnp.dot(value, wgu[l, 1 - c, n], preferred_element_type=F32)
            sent[s, n] = done.reshape(4, 2, ROWS, HALF).astype(sent.dtype)
            remote(sent.at[s, n], landed.at[s, n], c_s, (l, s, n), other_core)
        for n in (1, 0):
            done = jnp.dot(value, wgu[l, c, n], preferred_element_type=F32)
            pown[s, n] = done.reshape(4, 2, ROWS, HALF)

    def scatter(l, s, n):
        landed = core_buffers[l][1]
        wait_bytes(landed.at[s, n], c_s.at[1, l, s, n])
        if n == 0:
            for j, side in enumerate((1 - yl, yl)):
                total = pown[s, 0, :, side] + landed[s, 0, :, side].astype(F32)
                xsend[l, s, j] = total.astype(BF16)
                for dx in ALONG_X:
                    remote(xsend.at[l, s, j, x_at[dx]], xrecv.at[l, s, j, dx - 1], r_s, (l, s, j), x_device[dx])
                pown[s, 0, :, side] = total
        else:
            for j in range(2):
                for i in (2 * j, 2 * j + 1):
                    at = x_at[(*ALONG_X, 0)[i]]
                    ysend[l, s, i] = (pown[s, 1, at, 1 - yl] + landed[s, 1, at, 1 - yl].astype(F32)).astype(BF16)
                two = pl.ds(2 * j, 2)
                remote(ysend.at[l, s, two], yback.at[l, s, two], r_s, (l, s, 2 + j), other_y)
            pown[s, 1, :, yl] = pown[s, 1, :, yl] + landed[s, 1, :, yl].astype(F32)

    def middle_gate(l, s, j):
        wait_bytes(xrecv.at[l, s, j], r_s.at[1, l, s, j])
        total = pown[s, 0, x, (1 - yl, yl)[j]]
        for t in range(3):
            total = total + xrecv[l, s, j, t].astype(F32)
        if j == 0:
            msend[l, s] = total.astype(BF16)
            remote(msend.at[l, s], mrecv.at[l, s], m_s, (l, s, 0), other_y)
        else:
            mown[s, 0] = total

    def middle_up(l, s, j):
        two = pl.ds(2 * j, 2)
        wait_bytes(yback.at[l, s, two], r_s.at[1, l, s, 2 + j])
        for i in (2 * j, 2 * j + 1):
            dx = (*ALONG_X, 0)[i]
            total = pown[s, 1, x_at[dx], yl] + yback[l, s, i].astype(F32)
            if dx > 0:
                nsend[l, s, i] = total.astype(BF16)
                remote(nsend.at[l, s, i], nrecv.at[l, s, i], m_s, (l, s, 1), x_device[dx])
            else:
                mown[s, 1] = total

    def activate(l, s):
        wait_bytes(mrecv.at[l, s], m_s.at[1, l, s, 0])
        gate = mown[s, 0] + mrecv[l, s].astype(F32)
        wait_bytes(nrecv.at[l, s], m_s.at[1, l, s, 1])
        up = mown[s, 1]
        for t in range(3):
            up = up + nrecv[l, s, t].astype(F32)
        hid[l, s, c, chip] = (gate / (1.0 + jnp.exp(-gate)) * up).astype(BF16)
        mine = hid.at[l, s, c, chip]
        for device in chip_device:
            remote(mine, mine, a_s, (l, s), device)

    def half_down(l, s, k):
        value = hid[l, s, k].reshape(8 * ROWS, HALF)
        return jnp.dot(value, wd[l, k], preferred_element_type=F32).reshape(8, ROWS, WIDTH)

    def forward(l, s):
        wait_bytes(hid.at[l, s, 0, pl.ds(0, 7)], a_s.at[1, l, s])
        rows = hid.at[l, s, c]
        remote(rows, rows, f_s, (l, s), other_core)
        if s == 0:
            for k in range(2):
                wait_bytes(wd.at[l, k], w_s.at[l, 1, k, 0])
        acc[s] = half_down(l, s, c)

    def down(l, s):
        wait_bytes(hid.at[l, s, 0], f_s.at[1, l, s])
        done = acc[s] + half_down(l, s, 1 - c)
        acc[s] = done
        zsend[l, s] = done.astype(BF16)
        for dz in ALONG_Z:
            remote(zsend.at[l, s, z_at[dz]], zrecv.at[l, s, dz - 1], z_s, (l, s), z_device[dz])

    def reduce_z(l, s):
        wait_bytes(zrecv.at[l, s], z_s.at[1, l, s])
        total = acc[s, z]
        for n in range(7):
            total = total + zrecv[l, s, n].astype(F32)
        ysum[l, s] = total
        remote(ysum.at[l, s], yrecv.at[l, s], y_s, (l, s), other_half)

    def gather_z(l, s):
        h, q = PARTS[s]
        wait_bytes(yrecv.at[l, s], y_s.at[1, l, s])
        total = ysum[l, s] + yrecv[l, s]
        if l == 0:
            tok[1, h, q, z] = total.astype(BF16)
            mine = tok.at[1, h, q, z]
            for dz in ALONG_Z:
                remote(mine, mine, t_s, (s,), z_device[dz])
        else:

            @pl.when(yh == q)
            def _():
                out[pl.ds(ROWS * h, ROWS), :] = total

    steps = {
        "gate_up": gate_up,
        "scatter0": lambda l, s: scatter(l, s, 0),
        "scatter1": lambda l, s: scatter(l, s, 1),
        "gate0": lambda l, s: middle_gate(l, s, 0),
        "gate1": lambda l, s: middle_gate(l, s, 1),
        "up0": lambda l, s: middle_up(l, s, 0),
        "up1": lambda l, s: middle_up(l, s, 1),
        "activate": activate,
        "forward": forward,
        "down": down,
        "reduce_z": reduce_z,
        "gather_z": gather_z,
    }
    first_send(0)
    first_own(0)
    first_send(1)
    first_forward(0)
    first_own(1)
    first_forward(1)
    def drain():
        for h in range(2):
            wait_bytes(tok.at[0, h, 0, 0], i_s.at[0, 0, h])
            for n in (1, 2):
                wait_bytes(tok.at[0, h, 0, pl.ds(0, 7)], i_s.at[0, n, h])
        for s in range(4):
            h, q = PARTS[s]
            wait_bytes(tok.at[1, h, q, pl.ds(0, 7)], t_s.at[0, s])
            for l in range(2):
                for n in range(2):
                    if l == 1:
                        wait_bytes(crecv2.at[s, n], c_s.at[0, l, s, n])
                    wait_bytes(xrecv.at[l, s, n], r_s.at[0, l, s, n])
                    wait_bytes(yback.at[l, s, pl.ds(0, 2)], r_s.at[0, l, s, 2 + n])
                    wait_bytes((mrecv, nrecv)[n].at[l, s], m_s.at[0, l, s, n])
                wait_bytes(hid.at[l, s, 0, pl.ds(0, 7)], a_s.at[0, l, s])
                wait_bytes(hid.at[l, s, 0], f_s.at[0, l, s])
                wait_bytes(zrecv.at[l, s], z_s.at[0, l, s])

    for n, (name, l, s) in enumerate(ORDER):
        if n == len(ORDER) - 1:
            drain()
        steps[name](l, s)
    for l in range(2):
        for s in range(4):
            wait_bytes(yrecv.at[l, s], y_s.at[0, l, s])


def shards(*arrays):
    vmem = pl.BlockSpec(memory_space=pltpu.VMEM)
    anywhere = pl.BlockSpec(memory_space=pl.ANY)
    L, S = 2, len(PARTS)
    sem = pltpu.SemaphoreType.DMA
    return pl.pallas_call(
        kernel,
        out_shape=jax.ShapeDtypeStruct((2 * ROWS, WIDTH), F32),
        in_specs=[vmem] + [anywhere] * 6,
        out_specs=vmem,
        scratch_shapes=[
            pltpu.VMEM((L, 2, 2, WIDTH, HALF), BF16),
            pltpu.VMEM((L, 2, HALF, WIDTH), BF16),
            pltpu.VMEM((L, 2, 2, 8, ROWS, WIDTH), BF16),
            pltpu.VMEM((S, 2, 4, 2, ROWS, HALF), F32),
            pltpu.VMEM((S, 2, 4, 2, ROWS, HALF), F32),
            pltpu.VMEM((S, 2, 4, 2, ROWS, HALF), F32),
            pltpu.VMEM((S, 2, 4, 2, ROWS, HALF), BF16),
            pltpu.VMEM((S, 2, 4, 2, ROWS, HALF), BF16),
            pltpu.VMEM((L, S, 2, 4, ROWS, HALF), BF16),
            pltpu.VMEM((L, S, 2, 3, ROWS, HALF), BF16),
            pltpu.VMEM((L, S, 4, ROWS, HALF), BF16),
            pltpu.VMEM((L, S, 4, ROWS, HALF), BF16),
            pltpu.VMEM((L, S, ROWS, HALF), BF16),
            pltpu.VMEM((L, S, ROWS, HALF), BF16),
            pltpu.VMEM((L, S, 3, ROWS, HALF), BF16),
            pltpu.VMEM((L, S, 3, ROWS, HALF), BF16),
            pltpu.VMEM((S, 2, ROWS, HALF), F32),
            pltpu.VMEM((L, S, 2, 8, ROWS, HALF), BF16),
            pltpu.VMEM((S, 8, ROWS, WIDTH), F32),
            pltpu.VMEM((L, S, 8, ROWS, WIDTH), BF16),
            pltpu.VMEM((L, S, 7, ROWS, WIDTH), BF16),
            pltpu.VMEM((L, S, ROWS, WIDTH), F32),
            pltpu.VMEM((L, S, ROWS, WIDTH), F32),
            sem((L, 2, 2, 2)),
            sem((2, L, S, 2)),
            sem((2, L, S, 4)),
            sem((2, L, S, 2)),
            sem((2, L, S)),
            sem((2, L, S)),
            sem((2, L, S)),
            sem((2, L, S)),
            sem((2, S)),
            sem((2, 3, 2)),
        ],
        compiler_params=pltpu.CompilerParams(collective_id=0, has_side_effects=True, vmem_limit_bytes=56 * 2**20),
        cost_estimate=pl.CostEstimate(flops=6 * 2 * 512 * 512 * 1792, bytes_accessed=6 * 512 * 1792 * 2, transcendentals=0),
    )(*arrays)


def solution(mesh):
    weights = (P("gx", "gy"), P("gx", "gy"), P("gy", "gx"))
    in_specs = (P("gy", "gx"), *weights, *weights)
    return jax.shard_map(shards, mesh=mesh, in_specs=in_specs, out_specs=P("gy", "gx"), check_vma=False)
```

time: 111 us -> 105 us (0.946)
  Pallas kernels: 109 us -> 103 us
    pallas_call x1, Pallas kernels: 109 us -> 103 us  [shards(): pl.pallas_call(kernel, out_shape=jax.ShapeDtypeStruct((2 * ROWS, WIDTH),...]
where the time goes in v4:
time: 105 us; the launch traced here: 104 us
  Pallas kernels  103 us (98%)
  local copies, waits for them, and re-layouts  1.47 us (1%)
    pallas_call x1, Pallas kernels, shards(): pl.pallas_call(kernel, out_shape=jax.ShapeDtypeStruct((2 * ROWS, WIDTH),...  103 us

profile of v4, /device:TPU:1, one launch (start us, length us, event | category | flops | bytes accessed | tf_op | source)
XLA Modules:
  0.0 104.3 jit_solution(8478777513429195838)
XLA Ops:
  0.0 102.9 %shard_map.73 = f32[32,512]{1,0:T(8,128)} custom-call(bf16[32,512]{1,0:T(8,128)(2,1)} %tokens.1, bf16[512,1792]{1,0:T(8,128)(2,1)} %g0.1, bf16[512,1792]{1,0:T(8,128)(2,1)} %u0.1, bf16[1792,512]{1,0:T(8,128)(2,1)} %d0.1, bf16[512,1792]{1,0:T(8,128)(2,1)} %g1.1, bf16[512,1792]{1,0:T(8,128)(2,1)} %u1_.1, bf16[1792,512]{1,0:T(8,128)(2,1)} %d1.1), custom_call_target="tpu_custom_call" | custom-call | flops 5637144576 | bytes 11010048 | tf_op jit(solution)/shard_map/pallas_call | solution.py:288
  102.9 1.5 %copy.9 = f32[32,512]{1,0:T(8,128)} copy(f32[32,512]{1,0:T(8,128)} %shard_map.73) | data formatting | bytes 131072

commit v5 on v4

--- a/solution.py
+++ b/solution.py
@@ -15,30 +15,30 @@
 BF16 = jnp.bfloat16
 F32 = jnp.float32
 ORDER = (
-    ("gate_up", 0, 0), ("gate_up", 0, 1), ("scatter1", 0, 0), ("scatter0", 0, 0),
-    ("gate_up", 0, 2), ("up0", 0, 0), ("scatter1", 0, 1), ("scatter0", 0, 1),
-    ("up1", 0, 0), ("gate0", 0, 0), ("gate1", 0, 0), ("scatter0", 0, 2),
-    ("up0", 0, 1), ("scatter1", 0, 2), ("up1", 0, 1), ("gate_up", 0, 3),
-    ("activate", 0, 0), ("gate1", 0, 1), ("gate0", 0, 1), ("gate1", 0, 2),
-    ("up1", 0, 2), ("scatter1", 0, 3), ("up0", 0, 2), ("scatter0", 0, 3),
-    ("gate0", 0, 2), ("activate", 0, 1), ("forward", 0, 0), ("down", 0, 0),
-    ("up1", 0, 3), ("activate", 0, 2), ("gate1", 0, 3), ("up0", 0, 3),
-    ("gate0", 0, 3), ("forward", 0, 1), ("down", 0, 1), ("reduce_z", 0, 0),
-    ("forward", 0, 2), ("activate", 0, 3), ("down", 0, 2), ("gather_z", 0, 0),
-    ("forward", 0, 3), ("reduce_z", 0, 1), ("down", 0, 3), ("reduce_z", 0, 2),
-    ("gather_z", 0, 1), ("gate_up", 1, 0), ("gather_z", 0, 2), ("scatter1", 1, 0),
-    ("scatter0", 1, 0), ("reduce_z", 0, 3), ("up0", 1, 0), ("gate_up", 1, 1),
-    ("up1", 1, 0), ("gate0", 1, 0), ("scatter1", 1, 1), ("gather_z", 0, 3),
-    ("gate1", 1, 0), ("scatter0", 1, 1), ("gate_up", 1, 2), ("activate", 1, 0),
-    ("scatter1", 1, 2), ("gate0", 1, 1), ("scatter0", 1, 2), ("up1", 1, 1),
-    ("gate_up", 1, 3), ("up0", 1, 1), ("up0", 1, 2), ("gate1", 1, 1),
-    ("scatter0", 1, 3), ("scatter1", 1, 3), ("gate0", 1, 2), ("up1", 1, 2),
-    ("activate", 1, 1), ("up0", 1, 3), ("up1", 1, 3), ("gate1", 1, 2),
-    ("gate0", 1, 3), ("forward", 1, 0), ("activate", 1, 2), ("gate1", 1, 3),
-    ("down", 1, 0), ("activate", 1, 3), ("forward", 1, 1), ("down", 1, 1),
-    ("forward", 1, 2), ("down", 1, 2), ("forward", 1, 3), ("reduce_z", 1, 0),
-    ("down", 1, 3), ("reduce_z", 1, 1), ("gather_z", 1, 0), ("reduce_z", 1, 2),
-    ("reduce_z", 1, 3), ("gather_z", 1, 1), ("gather_z", 1, 2), ("gather_z", 1, 3),
+    ("gate_up", 0, 1), ("gate_up", 0, 0), ("scatter0", 0, 1), ("scatter1", 0, 1),
+    ("scatter0", 0, 0), ("scatter1", 0, 0), ("gate_up", 0, 2), ("up0", 0, 1),
+    ("gate_up", 0, 3), ("up1", 0, 1), ("gate1", 0, 1), ("gate0", 0, 1),
+    ("scatter1", 0, 2), ("scatter0", 0, 2), ("up0", 0, 0), ("activate", 0, 1),
+    ("up1", 0, 2), ("gate1", 0, 2), ("up1", 0, 0), ("up0", 0, 2),
+    ("gate0", 0, 0), ("scatter1", 0, 3), ("gate0", 0, 2), ("scatter0", 0, 3),
+    ("gate1", 0, 0), ("forward", 0, 1), ("activate", 0, 0), ("down", 0, 1),
+    ("up0", 0, 3), ("up1", 0, 3), ("gate1", 0, 3), ("gate0", 0, 3),
+    ("activate", 0, 2), ("forward", 0, 0), ("reduce_z", 0, 1), ("down", 0, 0),
+    ("activate", 0, 3), ("forward", 0, 2), ("gather_z", 0, 1), ("down", 0, 2),
+    ("forward", 0, 3), ("reduce_z", 0, 0), ("down", 0, 3), ("gate_up", 1, 1),
+    ("gather_z", 0, 0), ("scatter0", 1, 1), ("reduce_z", 0, 2), ("scatter1", 1, 1),
+    ("gather_z", 0, 2), ("gate0", 1, 1), ("reduce_z", 0, 3), ("up0", 1, 1),
+    ("gate_up", 1, 0), ("up1", 1, 1), ("scatter1", 1, 0), ("scatter0", 1, 0),
+    ("gather_z", 0, 3), ("gate1", 1, 1), ("activate", 1, 1), ("gate_up", 1, 2),
+    ("scatter1", 1, 2), ("up0", 1, 0), ("scatter0", 1, 2), ("up1", 1, 0),
+    ("gate_up", 1, 3), ("gate0", 1, 0), ("scatter1", 1, 3), ("scatter0", 1, 3),
+    ("up0", 1, 2), ("gate1", 1, 2), ("up1", 1, 2), ("forward", 1, 1),
+    ("gate1", 1, 0), ("up0", 1, 3), ("gate0", 1, 2), ("gate0", 1, 3),
+    ("up1", 1, 3), ("activate", 1, 0), ("down", 1, 1), ("activate", 1, 2),
+    ("gate1", 1, 3), ("activate", 1, 3), ("forward", 1, 0), ("down", 1, 0),
+    ("forward", 1, 2), ("down", 1, 2), ("forward", 1, 3), ("reduce_z", 1, 1),
+    ("down", 1, 3), ("reduce_z", 1, 0), ("gather_z", 1, 1), ("gather_z", 1, 0),
+    ("reduce_z", 1, 2), ("reduce_z", 1, 3), ("gather_z", 1, 2), ("gather_z", 1, 3),
 )
 
 
@@ -49,7 +49,7 @@
 def kernel(
     tokens, g0, u0, d0, g1, u1, d1, out,
     wgu, wd, tok, pown, pother, crecv, pother2, crecv2, xsend, xrecv, ysend, yback, msend, mrecv, nsend, nrecv, mown, hid, acc, zsend, zrecv, ysum, yrecv,
-    w_s, c_s, r_s, m_s, a_s, f_s, z_s, y_s, t_s, i_s,
+    b_s, w_s, c_s, r_s, m_s, a_s, f_s, z_s, y_s, t_s, i_s,
 ):
     gx, gy = lax.axis_index("gx"), lax.axis_index("gy")
     c, chip = lax.rem(gx, 2), gx // 2
@@ -76,6 +76,13 @@
     for device in partners:
         pl.semaphore_signal(barrier, inc=1, device_id=device, device_id_type=pl.DeviceIdType.MESH)
 
+    met = set()
+
+    def first(*what):
+        new = what not in met
+        met.add(what)
+        return new
+
     weights = ((g0, u0, d0), (g1, u1, d1))
     halves = [pl.ds(k * HALF, HALF) for k in range(2)]
 
@@ -87,10 +94,12 @@
         for k in range(2):
             pltpu.make_async_copy(down.at[halves[k], :], wd.at[l, k], w_s.at[l, 1, k, 0]).start()
 
+    for h in range(2):
+        pltpu.make_async_copy(tokens.at[pl.ds(ROWS * h, ROWS), :], tok.at[0, h, yh, z], b_s.at[h]).start()
     weight_copies(0)
     weight_copies(1)
     for h in range(2):
-        tok[0, h, yh, z] = tokens[pl.ds(ROWS * h, ROWS), :]
+        wait_bytes(tok.at[0, h, yh, z], b_s.at[h])
     pl.semaphore_wait(barrier, len(partners))
 
     def first_send(h):
@@ -113,7 +122,7 @@
     def gate_up(l, s):
         h, q = PARTS[s]
         if l == 0:
-            if q == 0:
+            if first(0, h):
                 for n in (1, 2):
                     wait_bytes(tok.at[0, h, 0, pl.ds(0, 7)], i_s.at[1, n, h])
         else:
@@ -121,7 +130,7 @@
             for n in range(2):
                 wait_bytes(crecv.at[s, n], c_s.at[0, 0, s, n])
         sent, landed = core_buffers[l]
-        if s == 0:
+        if first(1, l):
             for k in range(2):
                 for n in range(2):
                     wait_bytes(wgu.at[l, k, n], w_s.at[l, 0, k, n])
@@ -196,7 +205,7 @@
         wait_bytes(hid.at[l, s, 0, pl.ds(0, 7)], a_s.at[1, l, s])
         rows = hid.at[l, s, c]
         remote(rows, rows, f_s, (l, s), other_core)
-        if s == 0:
+        if first(2, l):
             for k in range(2):
                 wait_bytes(wd.at[l, k], w_s.at[l, 1, k, 0])
         acc[s] = half_down(l, s, c)
@@ -288,7 +297,7 @@
     return pl.pallas_call(
         kernel,
         out_shape=jax.ShapeDtypeStruct((2 * ROWS, WIDTH), F32),
-        in_specs=[vmem] + [anywhere] * 6,
+        in_specs=[anywhere] * 7,
         out_specs=vmem,
         scratch_shapes=[
             pltpu.VMEM((L, 2, 2, WIDTH, HALF), BF16),
@@ -314,6 +323,7 @@
             pltpu.VMEM((L, S, 7, ROWS, WIDTH), BF16),
             pltpu.VMEM((L, S, ROWS, WIDTH), F32),
             pltpu.VMEM((L, S, ROWS, WIDTH), F32),
+            sem((2,)),
             sem((L, 2, 2, 2)),
             sem((2, L, S, 2)),
             sem((2, L, S, 4)),

time: 105 us -> 104 us (level)
  no operation moved by 1% of the time
where the time goes in v5:
time: 104 us
  Pallas kernels  102 us (98%)
  local copies, waits for them, and re-layouts  1.47 us (1%)
    pallas_call x1, Pallas kernels, shards(): pl.pallas_call(kernel, out_shape=jax.ShapeDtypeStruct((2 * ROWS, WIDTH),...  102 us

profile of v5, /device:TPU:1, one launch (start us, length us, event | category | flops | bytes accessed | tf_op | source)
XLA Modules:
  0.0 104.0 jit_solution(10886147320875648220)
XLA Ops:
  0.0 102.5 %shard_map.73 = f32[32,512]{1,0:T(8,128)} custom-call(bf16[32,512]{1,0:T(8,128)(2,1)} %tokens.1, bf16[512,1792]{1,0:T(8,128)(2,1)} %g0.1, bf16[512,1792]{1,0:T(8,128)(2,1)} %u0.1, bf16[1792,512]{1,0:T(8,128)(2,1)} %d0.1, bf16[512,1792]{1,0:T(8,128)(2,1)} %g1.1, bf16[512,1792]{1,0:T(8,128)(2,1)} %u1_.1, bf16[1792,512]{1,0:T(8,128)(2,1)} %d1.1), custom_call_target="tpu_custom_call" | custom-call | flops 5637144576 | bytes 11010048 | tf_op jit(solution)/shard_map/pallas_call | solution.py:297
  102.5 1.5 %copy.9 = f32[32,512]{1,0:T(8,128)} copy(f32[32,512]{1,0:T(8,128)} %shard_map.73) | data formatting | bytes 131072

commit v6 on v4

--- a/solution.py
+++ b/solution.py
@@ -49,7 +49,7 @@
 def kernel(
     tokens, g0, u0, d0, g1, u1, d1, out,
     wgu, wd, tok, pown, pother, crecv, pother2, crecv2, xsend, xrecv, ysend, yback, msend, mrecv, nsend, nrecv, mown, hid, acc, zsend, zrecv, ysum, yrecv,
-    w_s, c_s, r_s, m_s, a_s, f_s, z_s, y_s, t_s, i_s,
+    b_s, w_s, c_s, r_s, m_s, a_s, f_s, z_s, y_s, t_s, i_s,
 ):
     gx, gy = lax.axis_index("gx"), lax.axis_index("gy")
     c, chip = lax.rem(gx, 2), gx // 2
@@ -71,10 +71,18 @@
     chip_device = [((x_at[dx] * 2 + lax.rem(yl + dy, 2)) * 2 + c, gy) for dx, dy in OFFSETS]
     z_at = [lax.rem(z + dz, 8) for dz in range(8)]
     z_device = [(gx, yh * 8 + to) for to in z_at]
-    partners = [z_device[dz] for dz in ALONG_Z] + [other_half] + chip_device + [other_core]
+    across = [(gx, (1 - yh) * 8 + z_at[dz]) for dz in (*ALONG_Z, 0)]
+    partners = across + [z_device[dz] for dz in ALONG_Z] + chip_device + [other_core]
     barrier = pltpu.get_barrier_semaphore()
     for device in partners:
         pl.semaphore_signal(barrier, inc=1, device_id=device, device_id_type=pl.DeviceIdType.MESH)
+
+    met = set()
+
+    def first(*what):
+        new = what not in met
+        met.add(what)
+        return new
 
     weights = ((g0, u0, d0), (g1, u1, d1))
     halves = [pl.ds(k * HALF, HALF) for k in range(2)]
@@ -87,41 +95,35 @@
         for k in range(2):
             pltpu.make_async_copy(down.at[halves[k], :], wd.at[l, k], w_s.at[l, 1, k, 0]).start()
 
+    for h in range(2):
+        pltpu.make_async_copy(tokens.at[pl.ds(ROWS * h, ROWS), :], tok.at[0, h, yh, z], b_s.at[h]).start()
     weight_copies(0)
     weight_copies(1)
     for h in range(2):
-        tok[0, h, yh, z] = tokens[pl.ds(ROWS * h, ROWS), :]
+        wait_bytes(tok.at[0, h, yh, z], b_s.at[h])
     pl.semaphore_wait(barrier, len(partners))
 
     def first_send(h):
         mine = tok.at[0, h, yh, z]
-        remote(mine, mine, i_s, (0, h), other_half)
-
-    def first_own(h):
-        mine = tok.at[0, h, yh, z]
+        for device in across:
+            remote(mine, mine, i_s, (0, h), device)
         for dz in ALONG_Z:
             remote(mine, mine, i_s, (1, h), z_device[dz])
-
-    def first_forward(h):
-        theirs = tok.at[0, h, 1 - yh, z]
-        wait_bytes(theirs, i_s.at[1, 0, h])
-        for dz in ALONG_Z:
-            remote(theirs, theirs, i_s, (2, h), z_device[dz])
 
     core_buffers = ((pother, crecv), (pother2, crecv2))
 
     def gate_up(l, s):
         h, q = PARTS[s]
         if l == 0:
-            if q == 0:
-                for n in (1, 2):
-                    wait_bytes(tok.at[0, h, 0, pl.ds(0, 7)], i_s.at[1, n, h])
+            if first(0, h):
+                wait_bytes(tok.at[0, h, 0, pl.ds(0, 7)], i_s.at[1, 1, h])
+                wait_bytes(tok.at[0, h, 0], i_s.at[1, 0, h])
         else:
             wait_bytes(tok.at[1, h, q, pl.ds(0, 7)], t_s.at[1, s])
             for n in range(2):
                 wait_bytes(crecv.at[s, n], c_s.at[0, 0, s, n])
         sent, landed = core_buffers[l]
-        if s == 0:
+        if first(1, l):
             for k in range(2):
                 for n in range(2):
                     wait_bytes(wgu.at[l, k, n], w_s.at[l, 0, k, n])
@@ -196,7 +198,7 @@
         wait_bytes(hid.at[l, s, 0, pl.ds(0, 7)], a_s.at[1, l, s])
         rows = hid.at[l, s, c]
         remote(rows, rows, f_s, (l, s), other_core)
-        if s == 0:
+        if first(2, l):
             for k in range(2):
                 wait_bytes(wd.at[l, k], w_s.at[l, 1, k, 0])
         acc[s] = half_down(l, s, c)
@@ -247,16 +249,11 @@
         "gather_z": gather_z,
     }
     first_send(0)
-    first_own(0)
     first_send(1)
-    first_forward(0)
-    first_own(1)
-    first_forward(1)
     def drain():
         for h in range(2):
-            wait_bytes(tok.at[0, h, 0, 0], i_s.at[0, 0, h])
-            for n in (1, 2):
-                wait_bytes(tok.at[0, h, 0, pl.ds(0, 7)], i_s.at[0, n, h])
+            wait_bytes(tok.at[0, h, 0], i_s.at[0, 0, h])
+            wait_bytes(tok.at[0, h, 0, pl.ds(0, 7)], i_s.at[0, 1, h])
         for s in range(4):
             h, q = PARTS[s]
             wait_bytes(tok.at[1, h, q, pl.ds(0, 7)], t_s.at[0, s])
@@ -288,7 +285,7 @@
     return pl.pallas_call(
         kernel,
         out_shape=jax.ShapeDtypeStruct((2 * ROWS, WIDTH), F32),
-        in_specs=[vmem] + [anywhere] * 6,
+        in_specs=[anywhere] * 7,
         out_specs=vmem,
         scratch_shapes=[
             pltpu.VMEM((L, 2, 2, WIDTH, HALF), BF16),
@@ -314,6 +311,7 @@
             pltpu.VMEM((L, S, 7, ROWS, WIDTH), BF16),
             pltpu.VMEM((L, S, ROWS, WIDTH), F32),
             pltpu.VMEM((L, S, ROWS, WIDTH), F32),
+            sem((2,)),
             sem((L, 2, 2, 2)),
             sem((2, L, S, 2)),
             sem((2, L, S, 4)),
@@ -323,7 +321,7 @@
             sem((2, L, S)),
             sem((2, L, S)),
             sem((2, S)),
-            sem((2, 3, 2)),
+            sem((2, 2, 2)),
         ],
         compiler_params=pltpu.CompilerParams(collective_id=0, has_side_effects=True, vmem_limit_bytes=56 * 2**20),
         cost_estimate=pl.CostEstimate(flops=6 * 2 * 512 * 512 * 1792, bytes_accessed=6 * 512 * 1792 * 2, transcendentals=0),

time: 105 us -> 103 us (0.981)
    pallas_call x1, Pallas kernels: 103 us -> 102 us  [shards(): pl.pallas_call(kernel, out_shape=jax.ShapeDtypeStruct((2 * ROWS, WIDTH),...]
where the time goes in v6:
time: 103 us
  Pallas kernels  102 us (99%)
  local copies, waits for them, and re-layouts  1.47 us (1%)
    pallas_call x1, Pallas kernels, shards(): pl.pallas_call(kernel, out_shape=jax.ShapeDtypeStruct((2 * ROWS, WIDTH),...  102 us

profile of v6, /device:TPU:1, one launch (start us, length us, event | category | flops | bytes accessed | tf_op | source)
XLA Modules:
  0.0 103.1 jit_solution(5403914072681644041)
XLA Ops:
  0.0 101.6 %shard_map.73 = f32[32,512]{1,0:T(8,128)} custom-call(bf16[32,512]{1,0:T(8,128)(2,1)} %tokens.1, bf16[512,1792]{1,0:T(8,128)(2,1)} %g0.1, bf16[512,1792]{1,0:T(8,128)(2,1)} %u0.1, bf16[1792,512]{1,0:T(8,128)(2,1)} %d0.1, bf16[512,1792]{1,0:T(8,128)(2,1)} %g1.1, bf16[512,1792]{1,0:T(8,128)(2,1)} %u1_.1, bf16[1792,512]{1,0:T(8,128)(2,1)} %d1.1), custom_call_target="tpu_custom_call" | custom-call | flops 5637144576 | bytes 11010048 | tf_op jit(solution)/shard_map/pallas_call | solution.py:285
  101.6 1.5 %copy.9 = f32[32,512]{1,0:T(8,128)} copy(f32[32,512]{1,0:T(8,128)} %shard_map.73) | data formatting | bytes 131072
